TPU v7x, 256 devices: a whole 4x4x8 slice. The times are simulated.
256 devices in a mesh: row: 16 (over z_hi, x, core), col: 16 (over y, z_lo).
Axes of the slice: x: 4, y: 4, z: 8 (z_hi: 2, z_lo: 4; z = z_hi * 4 + z_lo), core: 2. Of those that a mesh axis runs over, the one named last changes fastest.
Arguments:
- features: bfloat16 [131072, 128], P(('col', 'row')), may hold values from -240 to 240
- weight: bfloat16 [128, 256], replicated, may hold values from -0.5 to 0.5
- row_degree: int32 [131072], P(('row', 'col')), may hold values from 320 to 640
- col_degree: int32 [131072], P(('col', 'row')), may hold values from 320 to 640
- tile_cols: int32 [1024, 16, 6], P('row', 'col'), may hold values from 0 to 63, all different within a row
- slot_mask: int32 [1024, 16, 6], P('row', 'col'), may hold values 0 or 1
- tile_entries: bfloat16 [1024, 16, 6, 128, 128], P('row', 'col'), may hold values from 0 to 1, as said below
- cotangent: bfloat16 [131072, 256], P(('row', 'col')), may hold values from -192 to 192
Outputs:
- hidden: bfloat16 [131072, 256], P(('row', 'col'))
- weight_grad: float32 [128, 256], replicated
- feature_grad: bfloat16 [131072, 128], P(('col', 'row'))
Inputs may be any that keep to these rules, and one draw needn't show every extreme that they name: `tile_cols`: the 6 slots of each tile row and column block name different column tiles. `tile_entries`: every entry is 0 or 1.
All inputs are finite; a program needn't handle non-finite values. No bound on the sum of `slot_mask` on one device may be relied on, other than what follows from the above.
Results may differ from a plain program's by a relative error of at most 0.03.
Values may be sent and summed in bfloat16 or wider, within the bound.
A program may use at most 128 MiB of HBM per device.

v0:
```python
import math

import jax
import jax.numpy as jnp
from jax import lax
from jax.sharding import PartitionSpec as P


def body(features, weight, row_degree, col_degree, tile_cols, slot_mask, tile_entries, cotangent):
    tile_size = tile_entries.shape[-1]
    node_local, feat_width = features.shape
    col_scale = lax.rsqrt(col_degree.astype(jnp.float32))
    row_scale = lax.rsqrt(row_degree.astype(jnp.float32))
    scaled = (features.astype(jnp.float32) * col_scale[:, None]).astype(jnp.bfloat16)
    panel_rows = lax.all_gather(scaled, "row", axis=0, tiled=True)
    panel_tiles = panel_rows.reshape(-1, tile_size, feat_width)
    tile_index = tile_cols[:, 0, :]
    slot_live = slot_mask[:, 0, :]
    entries = tile_entries[:, 0]
    gathered = panel_tiles[tile_index] * slot_live[:, :, None, None].astype(jnp.bfloat16)
    product = jnp.einsum("rkab,rkbf->raf", entries, gathered, preferred_element_type=jnp.float32)
    aggregate = lax.psum_scatter(
        product.reshape(entries.shape[0] * tile_size, feat_width).astype(jnp.bfloat16),
        "col",
        scatter_dimension=0,
        tiled=True,
    ).astype(jnp.float32)
    smoothed = (aggregate * row_scale[:, None]).astype(jnp.bfloat16)
    pre_act = jnp.dot(smoothed, weight, preferred_element_type=jnp.float32)
    hidden = jax.nn.gelu(pre_act).astype(jnp.bfloat16)
    _, pull_back = jax.vjp(jax.nn.gelu, pre_act)
    grad_pre = pull_back(cotangent.astype(jnp.float32))[0].astype(jnp.bfloat16)
    local_weight = jnp.einsum("nf,nh->fh", smoothed, grad_pre, preferred_element_type=jnp.float32)
    node_count = node_local * lax.axis_size("row") * lax.axis_size("col")
    grad_smooth = (
        jnp.einsum("nh,fh->nf", grad_pre, weight, preferred_element_type=jnp.float32)
        * row_scale[:, None]
    ).astype(jnp.bfloat16)
    grad_rows = lax.all_gather(grad_smooth, "col", axis=0, tiled=True)
    grad_tiles = grad_rows.reshape(-1, tile_size, feat_width)
    contrib = jnp.einsum("rkab,raf->rkbf", entries, grad_tiles, preferred_element_type=jnp.float32)
    column_tiles = panel_tiles.shape[0]
    target = jnp.where(slot_live > 0, tile_index, column_tiles).reshape(-1)
    column_all = jax.ops.segment_sum(
        contrib.reshape(-1, tile_size, feat_width), target, num_segments=column_tiles + 1
    )
    column_all = column_all[:column_tiles].reshape(column_tiles * tile_size, feat_width)
    column_total = lax.psum_scatter(
        column_all.astype(jnp.bfloat16), "row", scatter_dimension=0, tiled=True
    ).astype(jnp.float32)
    feature_grad = (column_total * col_scale[:, None]).astype(jnp.bfloat16)
    weight_grad = lax.psum(local_weight, ("row", "col")) * (1.0 / (32.0 * math.sqrt(node_count)))
    return (hidden, weight_grad, feature_grad)


def solution(mesh):
    return jax.shard_map(
        body,
        mesh=mesh,
        in_specs=(
            P(("col", "row"), None),
            P(),
            P(("row", "col")),
            P(("col", "row")),
            P("row", "col", None),
            P("row", "col", None),
            P("row", "col", None, None, None),
            P(("row", "col"), None),
        ),
        out_specs=(P(("row", "col"), None), P(), P(("col", "row"), None)),
        check_vma=False,
    )
```

profile of v0, /device:TPU:1, one launch (start us, length us, event | category | flops | bytes accessed | tf_op | source)
XLA Modules:
  0.0 620.3 jit_solution(11518111010148497993)
XLA Ops:
  7.2 0.0 all-gather.3.cloned.1.call-start
  7.2 0.7 convert_rsqrt_fusion.1
  7.9 1.7 multiply_convert_fusion.3
  9.6 0.0 all-gather.3.cloned.1.call-update
  9.6 0.0 reduce-scatter.3.cloned.1.call-start
  9.7 0.7 compare_select_fusion
  10.4 0.1 copy.13
  10.5 0.1 reshape.86
  10.6 0.8 compare_select_fusion.1
  11.4 0.1 copy.20
  11.5 67.0 %all-gather.3.cloned.1.call-done = bf16[8192,128]{1,0:T(8,128)(2,1)} async-done(((bf16[512,128]{1,0:T(8,128)(2,1)}), bf16[8192,128]{1,0:T(8,128)(2,1)}) %all-gather.3.cloned.1.call-update) | async-done | bytes 2097168 | tf_op jit(solution)/shard_map/all_gather | solution.py:15
  78.5 12.9 %gather_fusion = bf16[384,128,128]{2,1,0:T(8,128)(2,1)} fusion(bf16[64,128,128]{2,1,0:T(8,128)(2,1)} %bitcast.37, s32[1024]{0:T(1024)S(1)} %pad_clamp_fusion), kind=kCustom, calls=%fused_computation | custom fusion | bytes 25167360 | tf_op jit(solution)/shard_map/gather | solution.py:20
  91.4 13.1 %bitcast_convert_fusion = bf16[64,128,128]{1,2,0:T(8,128)(2,1)} fusion(bf16[64,6,128,128]{3,2,1,0:T(8,128)(2,1)} %bitcast.38, bf16[64,6]{1,0:T(8,128)(2,1)S(1)} %bitcast.42, bf16[64,1,6,128,128]{4,3,2,1,0:T(8,128)(2,1)} %param.14), kind=kOutput, calls=%fused_computation.9 | convolution fusion | flops 1636827136 | bytes 27263744 | tf_op jit(solution)/shard_map/rkab,rkbf->raf/dot_general | solution.py:21
  104.5 0.0 all-gather.5.cloned.1.call-start
  104.6 76.4 %reduce-scatter.3.cloned.1.call-done = bf16[512,128]{1,0:T(8,128)(2,1)} async-done(((bf16[8192,128]{1,0:T(8,128)(2,1)}), bf16[512,128]{1,0:T(8,128)(2,1)}) %reduce-scatter.3.cloned.1.call-update) | async-done | bytes 131088 | tf_op jit(solution)/shard_map/reduce_scatter | solution.py:22
  180.9 2.2 fusion.13
  183.2 0.9 fusion.10
  184.1 0.0 all-reduce.2.cloned.1.call-start
  184.1 0.1 copy.15
  184.2 0.1 reshape.94
  184.4 1.9 fusion.21
  186.3 0.2 reduce-scatter.5.cloned.1.call-start
  186.5 82.8 %all-gather.5.cloned.1.call-done = bf16[8192,128]{1,0:T(8,128)(2,1)} async-done(((bf16[512,128]{1,0:T(8,128)(2,1)}), bf16[8192,128]{1,0:T(8,128)(2,1)}) %all-gather.5.cloned.1.call-update) | async-done | bytes 2097168 | tf_op jit(solution)/shard_map/all_gather | solution.py:39
  269.3 17.0 %fusion = f32[64,128,6,128]{3,1,2,0:T(8,128)} fusion(bf16[64,128,128,1]{2,1,3,0:T(8,128)(2,1)} %bitcast.40, bf16[64,1,6,128,128]{4,3,2,1,0:T(8,128)(2,1)} %param.14), kind=kOutput, calls=%fused_computation.2 | convolution fusion | flops 1610612736 | bytes 39845888 | tf_op jit(solution)/shard_map/rkab,raf->rkbf/dot_general | solution.py:41
  286.3 24.7 %copy.17 = f32[384,128,128]{2,1,0:T(8,128)} copy(f32[384,128,128]{1,2,0:T(8,128)} %bitcast.36) | data formatting | bytes 50331648 | tf_op jit(solution)/shard_map/reshape | solution.py:45
  311.0 2.5 broadcast_in_dim.3
  313.5 78.2 %scatter_fusion = f32[65,128,128]{2,1,0:T(8,128)} fusion(f32[65,128,128]{2,1,0:T(8,128)} %broadcast_in_dim.3, s32[384]{0:T(512)S(1)} %reshape.94, f32[384,128,128]{2,1,0:T(8,128)} %copy.17), kind=kCustom, calls=%fused_computation.1 | custom fusion | flops 6291456 | bytes 75499008 | tf_op jit(solution)/shard_map/scatter-add | solution.py:44
  391.7 3.9 slice.9
  395.7 128.7 %all-reduce.2.cloned.1.call-done = f32[128,256]{1,0:T(8,128)} async-done(((f32[128,256]{1,0:T(8,128)}), f32[128,256]{1,0:T(8,128)}) %all-reduce.2.cloned.1.call-update) | async-done | bytes 131088 | tf_op jit(solution)/shard_map/psum | solution.py:52
  524.4 1.6 broadcast_multiply_fusion
  525.9 86.1 %reduce-scatter.5.cloned.1.call-done = bf16[512,128]{1,0:T(8,128)(2,1)} async-done(((bf16[8192,128]{1,0:T(8,128)(2,1)}), bf16[512,128]{1,0:T(8,128)(2,1)}) %reduce-scatter.5.cloned.1.call-update) | async-done | bytes 131088 | tf_op jit(solution)/shard_map/reduce_scatter | solution.py:48
  612.1 1.7 multiply_convert_fusion.1
  (14 shorter events, 0.1 us)
Async XLA Ops:
  7.2 173.8 %copy-start = (bf16[128,256]{1,0:T(8,128)(2,1)S(1)}, bf16[128,256]{1,0:T(8,128)(2,1)}, u32[]{:S(2)}) copy-start(bf16[128,256]{1,0:T(8,128)(2,1)} %param.9) | copy-start | bytes 196612
  7.2 71.3 %all-gather.3.cloned.1.call-start = ((), (), s32[]{:S(2)}) async-start(), calls=%async_computation.2 | async-start | bytes 2228224 | tf_op jit(solution)/shard_map/all_gather | solution.py:15
  9.6 171.3 %reduce-scatter.3.cloned.1.call-start = ((), (), s32[]{:S(2)}) async-start(), calls=%async_computation.3 | async-start | bytes 2228224 | tf_op jit(solution)/shard_map/reduce_scatter | solution.py:22
  91.4 13.2 %copy-start.2 = (s32[512]{0:T(512)S(1)}, s32[512]{0:T(512)}, u32[]{:S(2)}) copy-start(s32[512]{0:T(512)} %param.10) | copy-start | bytes 6148
  91.4 89.6 %copy-start.3 = (bf16[512,256]{1,0:T(8,128)(2,1)S(1)}, bf16[512,256]{1,0:T(8,128)(2,1)}, u32[]{:S(2)}) copy-start(bf16[512,256]{1,0:T(8,128)(2,1)} %param.15) | copy-start | bytes 786436
  104.5 164.8 %all-gather.5.cloned.1.call-start = ((), (), s32[]{:S(2)}) async-start(), calls=%async_computation.5 | async-start | bytes 2228224 | tf_op jit(solution)/shard_map/all_gather | solution.py:39
  184.1 340.3 %all-reduce.2.cloned.1.call-start = ((), (), s32[]{:S(2)}) async-start(), calls=%async_computation.4 | async-start | bytes 262144 | tf_op jit(solution)/shard_map/psum | solution.py:52
  186.3 425.8 %reduce-scatter.5.cloned.1.call-start = ((), (), s32[]{:S(2)}) async-start(), calls=%async_computation.6 | async-start | bytes 2228224 | tf_op jit(solution)/shard_map/reduce_scatter | solution.py:48
  313.5 300.3 %copy-start.1 = (bf16[128,256]{1,0:T(8,128)(2,1)S(1)}, bf16[128,256]{1,0:T(8,128)(2,1)}, u32[]{:S(2)}) copy-start(bf16[128,256]{1,0:T(8,128)(2,1)} %param.9) | copy-start | bytes 196612
Sparse Core Ops, SparseCore 0:
  11.3 67.1 all-gather.2
  104.6 76.2 reduce-scatter.2
  184.2 85.0 all-gather.4
  275.3 249.0 all-reduce.1
  528.4 83.5 reduce-scatter.4
where the time goes:
time: 622 us; the launch traced here: 620 us
  waiting for transfers between devices  441 us (71%)
  other arithmetic  85.3 us (14%)
  local copies, waits for them, and re-layouts  44.6 us (7%)
  matrix products  35.1 us (6%)
  between operations  13.8 us (2%)
    psum x1, waiting for transfers between devices, body(): lax.psum(local_weight, ('row', 'col'))  129 us
    reduce_scatter x1, waiting for transfers between devices, body(): lax.psum_scatter(column_all.astype(jnp.bfloat16), 'row', scatter_dimensio...  86.1 us
    all_gather x1, waiting for transfers between devices, body(): grad_rows = lax.all_gather(grad_smooth, 'col', axis=0, tiled=True)  82.8 us
    scatter-add x1, other arithmetic, body(): jax.ops.segment_sum(contrib.reshape(-1, tile_size, feat_width), target, n...  78.2 us
    reduce_scatter x1, waiting for transfers between devices, body(): lax.psum_scatter(product.reshape(entries.shape[0] * tile_size, feat_width...  76.4 us
    all_gather x1, waiting for transfers between devices, body(): panel_rows = lax.all_gather(scaled, 'row', axis=0, tiled=True)  67 us
    reshape x1, local copies, waits for them, and re-layouts, body(): contrib.reshape(-1, tile_size, feat_width)  24.7 us
    dot_general x1, matrix products, body(): jnp.einsum('rkab,raf->rkbf', entries, grad_tiles, preferred_element_type=...  17 us
  transfers between devices with their start and end apart: 5, of which 5 were waited for; matrix products, arithmetic and copies ran while one was open for 21% of the time, Pallas kernels for 0%

commit v1 on v0

v1 whole, which is shorter than its diff:
```python
import functools
import math

import jax
import jax.numpy as jnp
from jax import lax
from jax.experimental import pallas as pl
from jax.experimental.pallas import tpu as pltpu
from jax.sharding import PartitionSpec as P

MESH = pl.DeviceIdType.MESH
BF = jnp.bfloat16
F32 = jnp.float32

T = 128
B = 4
K = 6
TILES = 64
SLOTS = TILES * K
EMPTY = SLOTS
ZERO = TILES
FWD_ORDER = (2, 1, 3, 0)
BWD_ORDER = (0, 1, 3, 2)
N_COPIES = 160


def coords():
    row, col = lax.axis_index("row"), lax.axis_index("col")
    return row // 8, lax.rem(row // 2, 4), lax.rem(row, 2), col // 4, lax.rem(col, 4)


def mod4(value):
    return lax.rem(value + 8, 4)


class Copies:
    def __init__(self, send_sems, recv_sems):
        self.sems = (send_sems, recv_sems)
        self.made = []
        self.place = coords()

    def device(self, x=0, y=0, z=0, core=0, half=0):
        mz, mx, mc, my, ml = self.place
        row = lax.rem(mz + half, 2) * 8 + mod4(mx + x) * 2 + lax.rem(mc + core, 2)
        return (row, mod4(my + y) * 4 + mod4(ml + z))

    def send(self, src, dst, **shift):
        n = len(self.made)
        copy = pltpu.make_async_remote_copy(
            src_ref=src,
            dst_ref=dst,
            send_sem=self.sems[0].at[n],
            recv_sem=self.sems[1].at[n],
            device_id=self.device(**shift),
            device_id_type=MESH,
        )
        copy.start()
        self.made.append(copy)
        return copy


PEERS = (
    [dict(x=1), dict(x=3), dict(x=2)]
    + [dict(y=1), dict(y=3), dict(y=2)]
    + [dict(z=1), dict(z=3), dict(z=2)]
    + [dict(core=1), dict(half=1)]
)


def blocks(ref, first, count):
    return ref.at[pl.ds(first, count)]


def kernel(
    grad_scale,
    index_ref, prev_ref, last_ref, entries_hbm, feat_ref, weight_ref, rowdeg_ref, coldeg_ref, cot_ref,
    hidden_ref, wgrad_ref, fgrad_ref,
    entries, panel, parts, up1, down1, up2, down2, zsend, zrecv, total,
    gpanel, chain, wlocal, wy, wz, wx, wc, wh, wfull,
    csend, crecv, xsum, xup1, xdown1, xup2, xdown2, hsend, hrecv,
    load_sems, send_sems, recv_sems,
):
    net = Copies(send_sems, recv_sems)
    mz, mx, mc, my, ml = net.place
    row, col = lax.axis_index("row"), lax.axis_index("col")

    n_loads = 8
    share = TILES // n_loads
    loads = []
    for n in range(n_loads):
        load = pltpu.make_async_copy(
            entries_hbm.at[pl.ds(n * share, share)], entries.at[pl.ds(n * share, share)], load_sems.at[n]
        )
        load.start()
        loads.append(load)

    barrier = pltpu.get_barrier_semaphore()
    for shift in PEERS:
        pl.semaphore_signal(barrier, inc=1, device_id=net.device(**shift), device_id_type=MESH)

    col_scale = lax.rsqrt(coldeg_ref[...].astype(F32))
    row_scale = lax.rsqrt(rowdeg_ref[...].astype(F32))

    def down_rows(scale, t):
        return jnp.broadcast_to(scale[t : t + 1, :], (T, T)).T

    mine = row * B
    for t in range(B):
        panel[mine + t] = (feat_ref[pl.ds(t * T, T), :].astype(F32) * down_rows(col_scale, t)).astype(BF)
    panel[ZERO] = jnp.zeros((T, T), BF)
    chain[EMPTY] = jnp.zeros((T, T), F32)
    pl.semaphore_wait(barrier, len(PEERS))

    def panel_at(half, x, first=0, count=B):
        place = lax.rem(mz + half, 2) * 8 + mod4(mx + x) * 2 + mc
        return blocks(panel, place * B + first, count)

    def pass_on(part, dx, first, count, **shift):
        ref = panel_at(part, dx, first, count)
        return net.send(ref, ref, **shift)

    from_core = []

    def share_core(half, x, first=0, count=B):
        from_core.append(pass_on(half, x, first, count, core=1))

    over = [pass_on(0, 0, t, 1, half=1) for t in range(B)]
    right = pass_on(0, 0, 0, B, x=1)
    left = pass_on(0, 0, 0, B, x=3)
    share_core(0, 0)
    right.wait_recv()
    fright = pass_on(0, -1, 0, 2, x=1)
    left.wait_recv()
    fleft = pass_on(0, 1, 2, 2, x=3)
    share_core(0, -1)
    share_core(0, 1)
    rights, lefts = [], []
    for t in range(B):
        over[t].wait_recv()
        rights.append(pass_on(1, 0, t, 1, x=1))
        lefts.append(pass_on(1, 0, t, 1, x=3))
    share_core(1, 0)
    fright.wait_recv()
    fleft.wait_recv()
    share_core(0, 2)
    frights, flefts = [], []
    for t in range(B):
        rights[t].wait_recv()
        if t < 2:
            frights.append(pass_on(1, -1, t, 1, x=1))
        lefts[t].wait_recv()
        if t >= 2:
            flefts.append(pass_on(1, 1, t, 1, x=3))
    share_core(1, -1)
    share_core(1, 1)
    for copy in frights + flefts:
        copy.wait_recv()
    share_core(1, 2)
    for load in loads:
        load.wait()
    for copy in from_core:
        copy.wait_recv()

    def product(y, z):
        first = (mod4(my + y) * 4 + mod4(ml + z)) * B

        def tile(t, carry):
            r = first + t
            acc = jnp.zeros((T, T), F32)
            for k in range(0, K, 2):
                lhs = jnp.concatenate([entries[r, k], entries[r, k + 1]], axis=1)
                rhs = jnp.concatenate(
                    [panel[index_ref[r * K + k]], panel[index_ref[r * K + k + 1]]], axis=0
                )
                acc = acc + jnp.dot(lhs, rhs, preferred_element_type=F32)
            parts[r] = acc.astype(BF)
            return carry

        lax.fori_loop(0, B, tile, 0)
        return first

    def add_to(ref, first, count, other):
        where = pl.ds(first, count)
        ref[where] = (ref[where].astype(F32) + other.astype(F32)).astype(BF)

    ups1, downs1, ups2, downs2, zs = [], [], [], [], []
    for q in range(4):
        first = product(2, FWD_ORDER[q])
        ups1.append(net.send(blocks(parts, first, 2), up1.at[q], y=1))
        downs1.append(net.send(blocks(parts, first + 2, 2), down1.at[q], y=3))
    for q in range(4):
        first = product(1, FWD_ORDER[q])
        ups1[q].wait_recv()
        add_to(parts, first, 2, up1[q])
        ups2.append(net.send(blocks(parts, first, B), up2.at[q], y=1))
        first = product(3, FWD_ORDER[q])
        downs1[q].wait_recv()
        add_to(parts, first + 2, 2, down1[q])
        downs2.append(net.send(blocks(parts, first, B), down2.at[q], y=3))
    firsts = [product(0, FWD_ORDER[q]) for q in range(4)]
    for q in range(4):
        ups2[q].wait_recv()
        downs2[q].wait_recv()
        here = parts[pl.ds(firsts[q], B)].astype(F32) + up2[q].astype(F32) + down2[q].astype(F32)
        if q < 3:
            zsend[q] = here.astype(BF)
            zs.append(net.send(zsend.at[q], zrecv.at[q], z=FWD_ORDER[q]))
        else:
            total[...] = here
    for copy in zs:
        copy.wait_recv()

    weight = weight_ref[...]
    lean = math.sqrt(2.0 / math.pi)
    for t in range(B):
        rows = pl.ds(t * T, T)
        aggregate = total[t]
        for q in range(3):
            aggregate = aggregate + zrecv[q, t].astype(F32)
        smoothed = (aggregate * down_rows(row_scale, t)).astype(BF)
        pre = jnp.dot(smoothed, weight, preferred_element_type=F32)
        square = pre * pre
        slope = jnp.tanh(lean * pre * (1.0 + 0.044715 * square))
        gate = 0.5 * (1.0 + slope)
        hidden_ref[rows, :] = (pre * gate).astype(BF)
        steep = gate + 0.5 * pre * (1.0 - slope * slope) * (lean * (1.0 + 3.0 * 0.044715 * square))
        grad_pre = (cot_ref[rows, :].astype(F32) * steep).astype(BF)
        spread = lax.dot_general(weight, grad_pre, (((1,), (1,)), ((), ())), preferred_element_type=F32)
        gpanel[col * B + t] = (spread * row_scale[t : t + 1, :]).astype(BF)
        outer = lax.dot_general(smoothed, grad_pre, (((0,), (0,)), ((), ())), preferred_element_type=F32)
        if t == 0:
            wlocal[...] = outer
        else:
            wlocal[...] += outer

    def grads_at(y, z, first=0, count=B):
        place = mod4(my + y) * 4 + mod4(ml + z)
        return blocks(gpanel, place * B + first, count)

    def hand_on(dy, dz, first, count, **shift):
        ref = grads_at(dy, dz, first, count)
        return net.send(ref, ref, **shift)

    def back(y, z):
        first = (mod4(my + y) * 4 + mod4(ml + z)) * B

        def tile(t, carry):
            r = first + t
            grads = gpanel[r]
            for k in range(0, K, 2):
                slot = r * K + k
                rhs = jnp.concatenate([entries[r, k], entries[r, k + 1]], axis=1)
                both = jnp.dot(grads, rhs, preferred_element_type=F32)
                one = chain[prev_ref[slot]] + both[:, :T]
                two = chain[prev_ref[slot + 1]] + both[:, T:]
                chain[slot] = one
                chain[slot + 1] = two
            return carry

        lax.fori_loop(0, B, tile, 0)

    gups, gdowns, fups, fdowns = [], [], [], []
    gups.append(hand_on(0, 0, 0, B, y=1))
    gdowns.append(hand_on(0, 0, 0, B, y=3))
    gz = [None] + [hand_on(0, 0, 0, B, z=-BWD_ORDER[q]) for q in (1, 2, 3)]
    wys = [
        net.send(wlocal.at[pl.ds(mod4(my + d) * 32, 32)], wy.at[d - 1], y=d) for d in (1, 2, 3)
    ]
    back(0, 0)
    for q in range(4):
        off = BWD_ORDER[q]
        if q < 3:
            nxt = BWD_ORDER[q + 1]
        gups[q].wait_recv()
        fups.append(hand_on(-1, off, 0, 2, y=1))
        gdowns[q].wait_recv()
        fdowns.append(hand_on(1, off, 2, 2, y=3))
        if q < 3:
            gz[q + 1].wait_recv()
            gups.append(hand_on(0, nxt, 0, B, y=1))
            gdowns.append(hand_on(0, nxt, 0, B, y=3))
        back(-1, off)
        back(1, off)
        if q < 3:
            back(0, nxt)
        if q == 0:
            for copy in wys:
                copy.wait_recv()
            wz[3] = wlocal[pl.ds(my * 32, 32), :] + wy[0] + wy[1] + wy[2]
            wzs = [
                net.send(wz.at[3, pl.ds(mod4(ml + d) * 8, 8)], wz.at[d - 1, pl.ds(0, 8)], z=d) for d in (1, 2, 3)
            ]
        if q == 1:
            for copy in wzs:
                copy.wait_recv()
            wx[mx] = wz[3, pl.ds(ml * 8, 8), :] + wz[0, :8, :] + wz[1, :8, :] + wz[2, :8, :]
            wxs = [net.send(wx.at[mx], wx.at[mx], x=d) for d in (1, 2, 3)]
        if q == 2:
            for copy in wxs:
                copy.wait_recv()
            wc[0] = wx[0] + wx[1] + wx[2] + wx[3]
            wcs = net.send(wc.at[0], wc.at[1], core=1)
        if q == 3:
            wcs.wait_recv()
            wh[0] = wc[0] + wc[1]
            whs = net.send(wh.at[0], wh.at[1], half=1)
        fups[q].wait_recv()
        fdowns[q].wait_recv()
        back(2, off)

    def column(half, x, core):
        return (lax.rem(mz + half, 2) * 8 + mod4(mx + x) * 2 + lax.rem(mc + core, 2)) * B

    order = [(half, x) for half in (1, 0) for x in (2, 1, 3, 0)]
    cores = []
    for n, (half, x) in enumerate(order):
        first = column(half, x, 1)
        for t in range(B):
            csend[n, t] = chain[last_ref[first + t]].astype(BF)
        cores.append(net.send(csend.at[n], crecv.at[n], core=1))
    xups1, xdowns1, xups2, xdowns2 = [], [], [], []

    def chip_sum(n):
        half, x = order[n]
        first = column(half, x, 0)
        cores[n].wait_recv()
        for t in range(B):
            xsum[n, t] = (chain[last_ref[first + t]] + crecv[n, t].astype(F32)).astype(BF)

    for h in range(2):
        chip_sum(4 * h)
        xups1.append(net.send(xsum.at[4 * h, pl.ds(0, 2)], xup1.at[h], x=1))
        xdowns1.append(net.send(xsum.at[4 * h, pl.ds(2, 2)], xdown1.at[h], x=3))
    for h in range(2):
        chip_sum(4 * h + 1)
        chip_sum(4 * h + 2)
        xups1[h].wait_recv()
        xsum[4 * h + 1, :2] = (xsum[4 * h + 1, :2].astype(F32) + xup1[h].astype(F32)).astype(BF)
        xups2.append(net.send(xsum.at[4 * h + 1], xup2.at[h], x=1))
        xdowns1[h].wait_recv()
        xsum[4 * h + 2, 2:] = (xsum[4 * h + 2, 2:].astype(F32) + xdown1[h].astype(F32)).astype(BF)
        xdowns2.append(net.send(xsum.at[4 * h + 2], xdown2.at[h], x=3))
        chip_sum(4 * h + 3)

    whs.wait_recv()
    wrows = my * 32 + ml * 8
    wfull[pl.ds(wrows, 8), :] = (wh[0] + wh[1]) * grad_scale
    wzs2 = [
        net.send(wfull.at[pl.ds(wrows, 8)], wfull.at[pl.ds(wrows, 8)], z=d) for d in (1, 2, 3)
    ]

    xups2[0].wait_recv()
    xdowns2[0].wait_recv()
    hsend[...] = (xsum[3].astype(F32) + xup2[0].astype(F32) + xdown2[0].astype(F32)).astype(BF)
    across = net.send(hsend, hrecv, half=1)
    for copy in wzs2:
        copy.wait_recv()
    wband = wfull.at[pl.ds(my * 32, 32)]
    wys2 = [net.send(wband, wband, y=d) for d in (1, 2, 3)]
    xups2[1].wait_recv()
    xdowns2[1].wait_recv()
    across.wait_recv()
    for t in range(B):
        tile = xsum[7, t].astype(F32) + xup2[1, t].astype(F32) + xdown2[1, t].astype(F32) + hrecv[t].astype(F32)
        fgrad_ref[pl.ds(t * T, T), :] = (tile * col_scale[t : t + 1, :]).T.astype(BF)
    for copy in wys2:
        copy.wait_recv()
    wgrad_ref[...] = wfull[...]
    for copy in net.made:
        copy.wait_send()


def chains(tile_cols, slot_mask):
    index = jnp.where(slot_mask[:, 0, :] > 0, tile_cols[:, 0, :], ZERO).reshape(SLOTS)
    col = lax.axis_index("col")
    my, ml = col // 4, lax.rem(col, 4)
    slot = jnp.arange(SLOTS, dtype=jnp.int32)
    r = slot // K
    dy = lax.rem(r // 16 - my + 4, 4)
    dz = lax.rem(lax.rem(r // 4, 4) - ml + 4, 4)
    turns = [(0, 0)]
    for q in range(4):
        turns += [(3, BWD_ORDER[q]), (1, BWD_ORDER[q])]
        if q < 3:
            turns.append((0, BWD_ORDER[q + 1]))
        turns.append((2, BWD_ORDER[q]))
    turn = jnp.zeros((SLOTS,), jnp.int32)
    for n, (y, z) in enumerate(turns):
        turn = jnp.where((dy == y) & (dz == z), n, turn)
    key = (turn * (B * K) + lax.rem(slot, B * K)) * 512 + slot
    same = (index[:, None] == index[None, :]) & (key[None, :] < key[:, None])
    prev = jnp.max(jnp.where(same, key[None, :], -1), axis=1)
    prev = jnp.where((prev >= 0) & (index < ZERO), lax.rem(prev, 512), EMPTY)
    tiles = jnp.arange(TILES, dtype=jnp.int32)
    last = jnp.max(jnp.where(index[None, :] == tiles[:, None], key[None, :], -1), axis=1)
    last = jnp.where(last >= 0, lax.rem(last, 512), EMPTY)
    return index, prev, last


def body(features, weight, row_degree, col_degree, tile_cols, slot_mask, tile_entries, cotangent):
    index, prev, last = chains(tile_cols, slot_mask)
    vmem = pl.BlockSpec(memory_space=pltpu.VMEM)
    smem = pl.BlockSpec(memory_space=pltpu.SMEM)
    nodes, hidden_width = cotangent.shape
    count = nodes * lax.axis_size("row") * lax.axis_size("col")
    grad_scale = 1.0 / (32.0 * math.sqrt(count))

    def tiles(*lead, dtype=BF):
        return pltpu.VMEM((*lead, T, T), dtype)

    def wide(*shape):
        return pltpu.VMEM((*shape, hidden_width), F32)

    return pl.pallas_call(
        functools.partial(kernel, grad_scale),
        out_shape=(
            jax.ShapeDtypeStruct((nodes, hidden_width), BF),
            jax.ShapeDtypeStruct((T, hidden_width), F32),
            jax.ShapeDtypeStruct((nodes, T), BF),
        ),
        in_specs=[smem] * 3 + [pl.BlockSpec(memory_space=pl.ANY)] + [vmem] * 5,
        out_specs=(vmem, vmem, vmem),
        scratch_shapes=[
            tiles(TILES, K), tiles(TILES + 1), tiles(TILES),
            tiles(4, 2), tiles(4, 2), tiles(4, B), tiles(4, B), tiles(3, B), tiles(3, B), tiles(B, dtype=F32),
            tiles(TILES), tiles(SLOTS + 1, dtype=F32),
            wide(T), wide(3, 32), wide(4, 32), wide(4, 8), wide(2, 8), wide(2, 8), wide(T),
            tiles(8, B), tiles(8, B), tiles(8, B),
            tiles(2, 2), tiles(2, 2), tiles(2, B), tiles(2, B), tiles(B), tiles(B),
            pltpu.SemaphoreType.DMA((8,)),
            pltpu.SemaphoreType.DMA((N_COPIES,)),
            pltpu.SemaphoreType.DMA((N_COPIES,)),
        ],
        compiler_params=pltpu.CompilerParams(
            collective_id=0, has_side_effects=True, vmem_limit_bytes=60 * 1024 * 1024
        ),
        name="graph_layer",
    )(
        index, prev, last, tile_entries.reshape(TILES, K, T, T), features, weight,
        row_degree.reshape(B, T), col_degree.reshape(B, T), cotangent,
    )


def solution(mesh):
    return jax.shard_map(
        body,
        mesh=mesh,
        in_specs=(
            P(("col", "row"), None),
            P(),
            P(("row", "col")),
            P(("col", "row")),
            P("row", "col", None),
            P("row", "col", None),
            P("row", "col", None, None, None),
            P(("row", "col"), None),
        ),
        out_specs=(P(("row", "col"), None), P(), P(("col", "row"), None)),
        check_vma=False,
    )
```

time: 622 us -> 115 us (0.18)
  waiting for transfers between devices: 441 us -> 0 us
  Pallas kernels: 0 us -> 107 us
  other arithmetic: 85.3 us -> 2.24 us
  local copies, waits for them, and re-layouts: 44.6 us -> 5.04 us
  matrix products: 35.1 us -> 0 us
  between operations: 13.8 us -> 0.67 us
    reduce_scatter x2 -> x0, waiting for transfers between devices: 163 us -> none  [the longest x1 86.1 us: body(): lax.psum_scatter(column_all.astype(jnp.bfloat16), 'row', scatter_dimensio...]
    all_gather x2 -> x0, waiting for transfers between devices: 150 us -> none  [the longest x1 82.8 us: body(): grad_rows = lax.all_gather(grad_smooth, 'col', axis=0, tiled=True)]
    psum x1 -> x0, waiting for transfers between devices: 129 us -> none  [body(): lax.psum(local_weight, ('row', 'col'))]
    pallas_call x0 -> x1, Pallas kernels: none -> 107 us  [body(): pl.pallas_call(functools.partial(kernel, grad_scale), out_shape=(jax.Shap...]
    scatter-add x1 -> x0, other arithmetic: 78.2 us -> none  [body(): jax.ops.segment_sum(contrib.reshape(-1, tile_size, feat_width), target, n...]
    dot_general x5 -> x0, matrix products: 35.1 us -> none  [the longest x1 17 us: body(): jnp.einsum('rkab,raf->rkbf', entries, grad_tiles, preferred_element_type=...]
    reshape x1 -> x0, local copies, waits for them, and re-layouts: 24.7 us -> none  [body(): contrib.reshape(-1, tile_size, feat_width)]
    gather x1 -> x0, local copies, waits for them, and re-layouts: 12.9 us -> none  [body(): panel_tiles[tile_index] * slot_live[:, :, None, None].astype(jnp.bfloat16)]
  transfers between devices with their start and end apart: 5 -> 0, of which waited for: 5 -> 0; matrix products, arithmetic and copies ran while one was open for 21% -> 0% of each run, Pallas kernels for 0% -> 0%
where the time goes in v1:
time: 115 us
  Pallas kernels  107 us (93%)
  local copies, waits for them, and re-layouts  5.04 us (4%)
  other arithmetic  2.24 us (2%)
    pallas_call x1, Pallas kernels, body(): pl.pallas_call(functools.partial(kernel, grad_scale), out_shape=(jax.Shap...  107 us
    unnamed x5, local copies, waits for them, and re-layouts  4.81 us

profile of v1, /device:TPU:1, one launch (start us, length us, event | category | flops | bytes accessed | tf_op | source)
XLA Modules:
  0.0 115.0 jit_solution(3432576897278106076)
XLA Ops:
  0.7 0.7 compare_select_fusion
  1.4 0.1 copy.12
  1.5 0.1 select_n.242.index_ref
  1.6 0.0 copy-start
  1.7 0.1 select_reduce_fusion.1
  1.8 0.3 select_reduce_fusion
  2.0 0.6 fusion.8.prev_ref
  2.6 0.5 compare_select_fusion.3.last_ref
  3.1 0.0 copy-done
  3.1 107.0 %graph_layer.1 = (bf16[512,256]{1,0:T(8,128)(2,1)}, f32[128,256]{1,0:T(8,128)}, bf16[512,128]{1,0:T(8,128)(2,1)}) custom-call(s32[384]{0:T(512)} %copy-done, s32[384]{0:T(512)} %fusion.8.prev_ref, s32[64]{0:T(128)} %compare_select_fusion.3.last_ref, bf16[64,6,128,128]{3,2,1,0:T(8,128)(2,1)} %bitcast.5, bf16[512,128]{1,0:T(8,128)(2,1)} %feat_ref.1, ...), custom_call_target="tpu_custom_call" | custom-call | tf_op jit(solution)/shard_map/graph_layer/pallas_call | solution.py:414
  110.1 1.7 %copy.16 = bf16[512,256]{1,0:T(8,128)(2,1)} copy(bf16[512,256]{1,0:T(8,128)(2,1)} %get-tuple-element.6) | data formatting | bytes 524288
  111.8 1.6 %copy.17 = f32[128,256]{1,0:T(8,128)} copy(f32[128,256]{1,0:T(8,128)} %get-tuple-element.7) | data formatting | bytes 262144
  113.4 1.6 %copy.18 = bf16[512,128]{1,0:T(8,128)(2,1)} copy(bf16[512,128]{1,0:T(8,128)(2,1)} %get-tuple-element.8) | data formatting | bytes 262144
  (1 shorter events, 0.0 us)
Async XLA Ops:
  1.6 1.5 %copy-start = (s32[384]{0:T(512)}, s32[384]{0:T(512)S(1)}, u32[]{:S(2)}) copy-start(s32[384]{0:T(512)S(1)} %select_n.242.index_ref) | copy-start | bytes 4612

commit v2 on v1

v2 whole, which is shorter than its diff:
```python
import functools
import math

import jax
import jax.numpy as jnp
from jax import lax
from jax.experimental import pallas as pl
from jax.experimental.pallas import tpu as pltpu
from jax.sharding import PartitionSpec as P

MESH = pl.DeviceIdType.MESH
BF = jnp.bfloat16
F32 = jnp.float32

T = 128
B = 4
K = 6
TILES = 64
SLOTS = TILES * K
EMPTY = SLOTS
ZERO = TILES
FWD_ORDER = (3, 2, 1, 0)
TURNS = ((0, 0), (0, 1), (3, 0), (1, 0), (0, 2), (0, 3), (3, 1), (1, 1), (3, 2), (1, 2), (3, 3), (1, 3))
TURNS += ((2, 0), (2, 1), (2, 2), (2, 3))
N_COPIES = 160
N_LOADS = 8
LAST = 6
INDEX = 8


def coords():
    row, col = lax.axis_index("row"), lax.axis_index("col")
    return row // 8, lax.rem(row // 2, 4), lax.rem(row, 2), col // 4, lax.rem(col, 4)


def mod4(value):
    return lax.rem(value + 8, 4)


def masked(z, mask):
    return (z, z + 1 - 2 * lax.rem(z, 2), mod4(z + 2), 3 - z)[mask]


class Copies:
    def __init__(self, send_sems, recv_sems):
        self.sems = (send_sems, recv_sems)
        self.made = []
        self.place = coords()

    def device(self, x=0, y=0, z=0, core=0, half=0):
        mz, mx, mc, my, ml = self.place
        row = lax.rem(mz + half, 2) * 8 + mod4(mx + x) * 2 + lax.rem(mc + core, 2)
        return (row, mod4(my + y) * 4 + masked(ml, z))

    def send(self, src, dst, **shift):
        n = len(self.made)
        copy = pltpu.make_async_remote_copy(
            src_ref=src,
            dst_ref=dst,
            send_sem=self.sems[0].at[n],
            recv_sem=self.sems[1].at[n],
            device_id=self.device(**shift),
            device_id_type=MESH,
        )
        copy.start()
        self.made.append(copy)
        return copy


PEERS = (
    [dict(x=1), dict(x=3), dict(x=2)]
    + [dict(y=1), dict(y=3), dict(y=2)]
    + [dict(z=1), dict(z=3), dict(z=2)]
    + [dict(core=1), dict(half=1)]
)


def blocks(ref, first, count):
    return ref.at[pl.ds(first, count)]


def kernel(
    grad_scale,
    cols_hbm, mask_hbm, entries_hbm, feat_hbm, weight_hbm, rowdeg_hbm, coldeg_hbm, cot_hbm,
    hidden_hbm, wgrad_hbm, fgrad_hbm,
    cols_ref, mask_ref, feat_ref, weight_ref, rowdeg_ref, coldeg_ref, cot_ref, hidden_ref, fgrad_ref, found, places,
    entries, panel, parts, up1, down1, up2, down2, zsend, zrecv, total,
    gpanel, chain, wlocal, wy, wz, wx, wc, wh, wfull,
    csend, crecv, xsum, xup1, xdown1, xup2, xdown2, hsend, hrecv,
    load_sems, io_sems, send_sems, recv_sems,
):
    net = Copies(send_sems, recv_sems)
    mz, mx, mc, my, ml = net.place
    row, col = lax.axis_index("row"), lax.axis_index("col")

    barrier = pltpu.get_barrier_semaphore()
    for shift in PEERS:
        pl.semaphore_signal(barrier, inc=1, device_id=net.device(**shift), device_id_type=MESH)

    moves = []

    def move(src, dst):
        copy = pltpu.make_async_copy(src, dst, io_sems.at[len(moves)])
        copy.start()
        moves.append(copy)
        return copy

    got_coldeg = move(coldeg_hbm, coldeg_ref)
    got_feat = move(feat_hbm, feat_ref)
    got_cols = move(cols_hbm, cols_ref)
    got_mask = move(mask_hbm, mask_ref)
    got_rowdeg = move(rowdeg_hbm, rowdeg_ref)
    got_weight = move(weight_hbm, weight_ref)
    got_cot = move(cot_hbm, cot_ref)
    share = TILES // N_LOADS
    loads = []
    for n in range(N_LOADS):
        load = pltpu.make_async_copy(
            entries_hbm.at[pl.ds(n * share, share)], entries.at[pl.ds(n * share, share)], load_sems.at[n]
        )
        load.start()
        loads.append(load)

    got_coldeg.wait()
    got_feat.wait()
    col_scale = lax.rsqrt(coldeg_ref[...].astype(F32))

    def down_rows(scale, t):
        return jnp.broadcast_to(scale[t : t + 1, :], (T, T)).T

    mine = row * B
    for t in range(B):
        panel[mine + t] = (feat_ref[pl.ds(t * T, T), :].astype(F32) * down_rows(col_scale, t)).astype(BF)
    panel[ZERO] = jnp.zeros((T, T), BF)
    chain[EMPTY] = jnp.zeros((T, T), F32)
    pl.semaphore_wait(barrier, len(PEERS))

    def panel_at(half, x, first=0, count=B):
        place = lax.rem(mz + half, 2) * 8 + mod4(mx + x) * 2 + mc
        return blocks(panel, place * B + first, count)

    def pass_on(part, dx, first, count, **shift):
        ref = panel_at(part, dx, first, count)
        return net.send(ref, ref, **shift)

    from_core = []

    def share_core(half, x, first=0, count=B):
        from_core.append(pass_on(half, x, first, count, core=1))

    halves = (0, 2)
    over = [pass_on(0, 0, t, 2, half=1) for t in halves]
    right = pass_on(0, 0, 0, B, x=1)
    left = pass_on(0, 0, 0, B, x=3)
    share_core(0, 0)

    got_cols.wait()
    got_mask.wait()
    find_places(cols_ref, mask_ref, found, my, ml)
    got_places = move(found, places)

    right.wait_recv()
    fright = pass_on(0, -1, 0, 2, x=1)
    left.wait_recv()
    fleft = pass_on(0, 1, 2, 2, x=3)
    share_core(0, -1)
    share_core(0, 1)
    others = []
    for t, copy in zip(halves, over):
        copy.wait_recv()
        others.append([pass_on(1, 0, t, 2, x=d) for d in (1, 3, 2)])
        share_core(1, 0, t, 2)
    fright.wait_recv()
    fleft.wait_recv()
    share_core(0, 2)
    for t, copies in zip(halves, others):
        for copy, d in zip(copies, (-1, 1, 2)):
            copy.wait_recv()
            share_core(1, d, t, 2)
    for load in loads:
        load.wait()
    for copy in from_core:
        copy.wait_recv()
    got_places.wait()

    def product(y, z):
        first = (mod4(my + y) * 4 + masked(ml, z)) * B

        def tile(r):
            acc = jnp.zeros((T, T), F32)
            for k in range(0, K, 2):
                lhs = jnp.concatenate([entries[r, k], entries[r, k + 1]], axis=1)
                rhs = jnp.concatenate(
                    [panel[places[INDEX + k, r]], panel[places[INDEX + k + 1, r]]], axis=0
                )
                acc = acc + jnp.dot(lhs, rhs, preferred_element_type=F32)
            parts[r] = acc.astype(BF)

        for t in range(B):
            tile(first + t)
        return first

    def add_to(ref, first, count, other):
        where = pl.ds(first, count)
        ref[where] = (ref[where].astype(F32) + other.astype(F32)).astype(BF)

    ups1, downs1, ups2, downs2, zs = [], [], [], [], []
    for q in range(4):
        first = product(2, FWD_ORDER[q])
        ups1.append(net.send(blocks(parts, first, 2), up1.at[q], y=1))
        downs1.append(net.send(blocks(parts, first + 2, 2), down1.at[q], y=3))
    def second(q):
        first = product(1, FWD_ORDER[q])
        ups1[q].wait_recv()
        add_to(parts, first, 2, up1[q])
        ups2.append(net.send(blocks(parts, first, B), up2.at[q], y=1))
        first = product(3, FWD_ORDER[q])
        downs1[q].wait_recv()
        add_to(parts, first + 2, 2, down1[q])
        downs2.append(net.send(blocks(parts, first, B), down2.at[q], y=3))

    def third(q):
        first = product(0, FWD_ORDER[q])
        ups2[q].wait_recv()
        downs2[q].wait_recv()
        here = parts[pl.ds(first, B)].astype(F32) + up2[q].astype(F32) + down2[q].astype(F32)
        if q < 3:
            zsend[q] = here.astype(BF)
            zs.append(net.send(zsend.at[q], zrecv.at[q], z=FWD_ORDER[q]))
        else:
            total[...] = here

    second(0)
    second(1)
    second(2)
    third(0)
    second(3)
    third(1)
    third(2)
    third(3)
    for copy in zs:
        copy.wait_recv()

    got_rowdeg.wait()
    got_weight.wait()
    got_cot.wait()
    row_scale = lax.rsqrt(rowdeg_ref[...].astype(F32))
    weight = weight_ref[...]
    lean = math.sqrt(2.0 / math.pi)
    for t in range(B):
        rows = pl.ds(t * T, T)
        aggregate = total[t]
        for q in range(3):
            aggregate = aggregate + zrecv[q, t].astype(F32)
        smoothed = (aggregate * down_rows(row_scale, t)).astype(BF)
        pre = jnp.dot(smoothed, weight, preferred_element_type=F32)
        square = pre * pre
        slope = jnp.tanh(lean * pre * (1.0 + 0.044715 * square))
        gate = 0.5 * (1.0 + slope)
        hidden_ref[rows, :] = (pre * gate).astype(BF)
        steep = gate + 0.5 * pre * (1.0 - slope * slope) * (lean * (1.0 + 3.0 * 0.044715 * square))
        grad_pre = (cot_ref[rows, :].astype(F32) * steep).astype(BF)
        spread = lax.dot_general(weight, grad_pre, (((1,), (1,)), ((), ())), preferred_element_type=F32)
        gpanel[col * B + t] = (spread * row_scale[t : t + 1, :]).astype(BF)
        outer = lax.dot_general(smoothed, grad_pre, (((0,), (0,)), ((), ())), preferred_element_type=F32)
        if t == 0:
            wlocal[...] = outer
        else:
            wlocal[...] += outer

    put_hidden = move(hidden_ref, hidden_hbm)

    def grads_at(y, z, first=0, count=B):
        place = mod4(my + y) * 4 + masked(ml, z)
        return blocks(gpanel, place * B + first, count)

    def hand_on(dy, dz, first, count, **shift):
        ref = grads_at(dy, dz, first, count)
        return net.send(ref, ref, **shift)

    def back(y, z):
        first = (mod4(my + y) * 4 + masked(ml, z)) * B

        def tile(r):
            grads = gpanel[r]
            for k in range(0, K, 2):
                slot = r * K + k
                rhs = jnp.concatenate([entries[r, k], entries[r, k + 1]], axis=1)
                both = jnp.dot(grads, rhs, preferred_element_type=F32)
                one = chain[places[k, r]] + both[:, :T]
                two = chain[places[k + 1, r]] + both[:, T:]
                chain[slot] = one
                chain[slot + 1] = two

        for t in range(B):
            tile(first + t)

    gups, gdowns, fups, fdowns = [], [], [], []

    def along(mask):
        gups.append(hand_on(0, mask, 0, B, y=1))
        gdowns.append(hand_on(0, mask, 0, B, y=3))

    def forward(mask):
        gups[mask].wait_recv()
        fups.append(hand_on(-1, mask, 0, 2, y=1))
        gdowns[mask].wait_recv()
        fdowns.append(hand_on(1, mask, 2, 2, y=3))

    along(0)
    gz = [None] + [hand_on(0, 0, 0, B, z=mask) for mask in (1, 2, 3)]
    wys = [
        net.send(wlocal.at[pl.ds(mod4(my + d) * 32, 32)], wy.at[d - 1], y=d) for d in (1, 2, 3)
    ]
    back(0, 0)
    gz[1].wait_recv()
    along(1)
    back(0, 1)
    forward(0)
    back(3, 0)
    back(1, 0)
    gz[2].wait_recv()
    along(2)
    back(0, 2)
    gz[3].wait_recv()
    along(3)
    back(0, 3)
    forward(1)
    for copy in wys:
        copy.wait_recv()
    wz[3] = wlocal[pl.ds(my * 32, 32), :] + wy[0] + wy[1] + wy[2]
    wzs = [
        net.send(wz.at[3, pl.ds(masked(ml, m) * 8, 8)], wz.at[m - 1, pl.ds(0, 8)], z=m) for m in (1, 2, 3)
    ]
    back(3, 1)
    back(1, 1)
    forward(2)
    back(3, 2)
    back(1, 2)
    forward(3)
    back(3, 3)
    back(1, 3)
    for copy in wzs:
        copy.wait_recv()
    wx[mx] = wz[3, pl.ds(ml * 8, 8), :] + wz[0, :8, :] + wz[1, :8, :] + wz[2, :8, :]
    wxs = [net.send(wx.at[mx], wx.at[mx], x=d) for d in (1, 2, 3)]
    for mask in range(4):
        fups[mask].wait_recv()
        fdowns[mask].wait_recv()
        back(2, mask)
    for copy in wxs:
        copy.wait_recv()
    wc[0] = wx[0] + wx[1] + wx[2] + wx[3]
    wcs = net.send(wc.at[0], wc.at[1], core=1)

    def column(half, x, core):
        return (lax.rem(mz + half, 2) * 8 + mod4(mx + x) * 2 + lax.rem(mc + core, 2)) * B

    order = [(half, x) for half in (1, 0) for x in (2, 1, 3, 0)]
    cores = []
    for n, (half, x) in enumerate(order):
        first = column(half, x, 1)
        for t in range(B):
            csend[n, t] = chain[places[LAST, first + t]].astype(BF)
        cores.append(net.send(csend.at[n], crecv.at[n], core=1))
    near, far = {}, {}

    def chip_sum(n):
        half, x = order[n]
        first = column(half, x, 0)
        cores[n].wait_recv()
        for t in range(B):
            xsum[n, t] = (chain[places[LAST, first + t]] + crecv[n, t].astype(F32)).astype(BF)

    def opposite(h, t):
        near[h, t] = (
            net.send(blocks(xsum.at[4 * h], t, 1), blocks(xup1.at[h], t // 2, 1), x=1),
            net.send(blocks(xsum.at[4 * h], t + 1, 1), blocks(xdown1.at[h], t // 2, 1), x=3),
        )

    def beside(h, t):
        up, down = near[h, t]
        up.wait_recv()
        right, left = xsum.at[4 * h + 1], xsum.at[4 * h + 2]
        right[t] = (right[t].astype(F32) + xup1[h, t // 2].astype(F32)).astype(BF)
        up = net.send(blocks(right, t, 2), blocks(xup2.at[h], t, 2), x=1)
        down.wait_recv()
        left[t + 1] = (left[t + 1].astype(F32) + xdown1[h, t // 2].astype(F32)).astype(BF)
        far[h, t] = (up, net.send(blocks(left, t, 2), blocks(xdown2.at[h], t, 2), x=3))

    def gathered(h, t):
        for copy in far[h, t]:
            copy.wait_recv()
        two = pl.ds(t, 2)
        return xsum[4 * h + 3, two].astype(F32) + xup2[h, two].astype(F32) + xdown2[h, two].astype(F32)

    across = []

    def cross(t):
        hsend[pl.ds(t, 2)] = gathered(0, t).astype(BF)
        across.append(net.send(blocks(hsend, t, 2), blocks(hrecv, t, 2), half=1))

    chip_sum(0)
    opposite(0, 0)
    opposite(0, 2)
    chip_sum(1)
    chip_sum(2)
    beside(0, 0)
    beside(0, 2)
    chip_sum(4)
    opposite(1, 0)
    opposite(1, 2)
    wcs.wait_recv()
    wh[0] = wc[0] + wc[1]
    whs = net.send(wh.at[0], wh.at[1], half=1)
    chip_sum(3)
    cross(0)
    chip_sum(5)
    chip_sum(6)
    beside(1, 0)
    cross(2)
    beside(1, 2)
    chip_sum(7)

    whs.wait_recv()
    wrows = my * 32 + ml * 8
    wfull[pl.ds(wrows, 8), :] = (wh[0] + wh[1]) * grad_scale
    wzs2 = [
        net.send(wfull.at[pl.ds(wrows, 8)], wfull.at[pl.ds(wrows, 8)], z=d) for d in (1, 2, 3)
    ]

    for copy in wzs2:
        copy.wait_recv()
    wband = wfull.at[pl.ds(my * 32, 32)]
    wys2 = [net.send(wband, wband, y=d) for d in (1, 2, 3)]
    for t, copy in zip(halves, across):
        here = gathered(1, t)
        copy.wait_recv()
        for u in range(2):
            tile = here[u] + hrecv[t + u].astype(F32)
            fgrad_ref[pl.ds((t + u) * T, T), :] = (tile * col_scale[t + u : t + u + 1, :]).T.astype(BF)
    put_fgrad = move(fgrad_ref, fgrad_hbm)
    for copy in wys2:
        copy.wait_recv()
    put_wgrad = move(wfull, wgrad_hbm)
    for copy in net.made:
        copy.wait_send()
    for put in (put_hidden, put_fgrad, put_wgrad):
        put.wait()


def find_places(cols_ref, mask_ref, found, my, ml):
    square = (TILES, TILES)

    def turn_of(r):
        dy = mod4(r // 16 - my)
        z = lax.rem(r // 4, 4)
        turn = jnp.zeros_like(r)
        for n, (y, mask) in enumerate(TURNS):
            turn = jnp.where((dy == y) & (z == masked(ml, mask)), n, turn)
        return turn * B + lax.rem(r, B)

    over = lax.broadcasted_iota(jnp.int32, square, 1)
    down = lax.broadcasted_iota(jnp.int32, square, 0)
    turn_over = turn_of(over[:1])
    turn_down = turn_of(down)
    index = [jnp.where(mask_ref[k] > 0, cols_ref[k], ZERO) for k in range(K)]
    index_down = [jnp.broadcast_to(index[k], square).T for k in range(K)]
    key_down = [turn_down * 512 + down * K + k for k in range(K)]

    def slot_of(key, live):
        return jnp.where(live & (key >= 0), lax.rem(key, 512), EMPTY)

    ahead = turn_down < turn_over
    for k in range(K):
        best = jnp.full(square, -1, jnp.int32)
        for j in range(K):
            best = jnp.maximum(best, jnp.where(index_down[j] == index[k], key_down[j], -1))
        key = jnp.max(jnp.where(ahead, best, -1), axis=0, keepdims=True)
        found[k : k + 1, :TILES] = slot_of(key, index[k] < ZERO)
        found[INDEX + k : INDEX + k + 1, :TILES] = index[k]
    best = jnp.full(square, -1, jnp.int32)
    for j in range(K):
        best = jnp.maximum(best, jnp.where(index_down[j] == over, key_down[j], -1))
    key = jnp.max(best, axis=0, keepdims=True)
    found[LAST : LAST + 1, :TILES] = slot_of(key, key >= 0)


def finish(*refs):
    n = len(refs) // 2
    for source, target in zip(refs[:n], refs[n:]):
        target[...] = source[...]


def body(features, weight, row_degree, col_degree, tile_cols, slot_mask, tile_entries, cotangent):
    anywhere = pl.BlockSpec(memory_space=pl.ANY)
    vmem = pl.BlockSpec(memory_space=pltpu.VMEM)
    nodes, hidden_width = cotangent.shape
    count = nodes * lax.axis_size("row") * lax.axis_size("col")
    grad_scale = 1.0 / (32.0 * math.sqrt(count))

    def tiles(*lead, dtype=BF):
        return pltpu.VMEM((*lead, T, T), dtype)

    def wide(*shape):
        return pltpu.VMEM((*shape, hidden_width), F32)

    shapes = (
        jax.ShapeDtypeStruct((nodes, hidden_width), BF),
        jax.ShapeDtypeStruct((T, hidden_width), F32),
        jax.ShapeDtypeStruct((nodes, T), BF),
    )
    results = pl.pallas_call(
        functools.partial(kernel, grad_scale),
        out_shape=shapes,
        in_specs=[anywhere] * 8,
        out_specs=(anywhere,) * 3,
        scratch_shapes=[
            pltpu.VMEM((K, 1, TILES), jnp.int32), pltpu.VMEM((K, 1, TILES), jnp.int32),
            pltpu.VMEM((nodes, T), BF), pltpu.VMEM((T, hidden_width), BF),
            pltpu.VMEM((B, T), jnp.int32), pltpu.VMEM((B, T), jnp.int32),
            pltpu.VMEM((nodes, hidden_width), BF), pltpu.VMEM((nodes, hidden_width), BF), pltpu.VMEM((nodes, T), BF),
            pltpu.VMEM((16, 128), jnp.int32), pltpu.SMEM((16, 128), jnp.int32),
            tiles(TILES, K), tiles(TILES + 1), tiles(TILES),
            tiles(4, 2), tiles(4, 2), tiles(4, B), tiles(4, B), tiles(3, B), tiles(3, B), tiles(B, dtype=F32),
            tiles(TILES), tiles(SLOTS + 1, dtype=F32),
            wide(T), wide(3, 32), wide(4, 32), wide(4, 8), wide(2, 8), wide(2, 8), wide(T),
            tiles(8, B), tiles(8, B), tiles(8, B),
            tiles(2, 2), tiles(2, 2), tiles(2, B), tiles(2, B), tiles(B), tiles(B),
            pltpu.SemaphoreType.DMA((N_LOADS,)),
            pltpu.SemaphoreType.DMA((16,)),
            pltpu.SemaphoreType.DMA((N_COPIES,)),
            pltpu.SemaphoreType.DMA((N_COPIES,)),
        ],
        compiler_params=pltpu.CompilerParams(
            collective_id=0, has_side_effects=True, vmem_limit_bytes=60 * 1024 * 1024
        ),
        name="graph_layer",
    )(
        tile_cols.transpose(2, 1, 0), slot_mask.transpose(2, 1, 0), tile_entries.reshape(TILES, K, T, T),
        features, weight, row_degree.reshape(B, T), col_degree.reshape(B, T), cotangent,
    )
    return pl.pallas_call(
        finish,
        out_shape=shapes,
        in_specs=[vmem] * 3,
        out_specs=(vmem,) * 3,
        name="results",
    )(*results)


def solution(mesh):
    return jax.shard_map(
        body,
        mesh=mesh,
        in_specs=(
            P(("col", "row"), None),
            P(),
            P(("row", "col")),
            P(("col", "row")),
            P("row", "col", None),
            P("row", "col", None),
            P("row", "col", None, None, None),
            P(("row", "col"), None),
        ),
        out_specs=(P(("row", "col"), None), P(), P(("col", "row"), None)),
        check_vma=False,
    )
```

time: 115 us -> 100 us (0.87)
  Pallas kernels: 107 us -> 99.8 us
  local copies, waits for them, and re-layouts: 5.04 us -> 0 us
  other arithmetic: 2.24 us -> 0 us
    pallas_call x1 -> x2, Pallas kernels: 107 us -> 99.8 us  [the longest x1 97.9 us: body(): pl.pallas_call(functools.partial(kernel, grad_scale), out_shape=shapes, i...]
    unnamed x5 -> x0, local copies, waits for them, and re-layouts: 4.81 us -> none
    select_n x3 -> x0, other arithmetic: 1.82 us -> none  [the longest x1 0.71 us: chains(): jnp.where(slot_mask[:, 0, :] > 0, tile_cols[:, 0, :], ZERO).reshape(SLOTS)]
where the time goes in v2:
time: 100 us
  Pallas kernels  99.8 us (100%)
    pallas_call x1, Pallas kernels, body(): pl.pallas_call(functools.partial(kernel, grad_scale), out_shape=shapes, i...  97.9 us

profile of v2, /device:TPU:1, one launch (start us, length us, event | category | flops | bytes accessed | tf_op | source)
XLA Modules:
  0.0 100.4 jit_solution(7961196314481325843)
XLA Ops:
  0.6 97.9 %graph_layer.1 = (bf16[512,256]{1,0:T(8,128)(2,1)}, f32[128,256]{1,0:T(8,128)}, bf16[512,128]{1,0:T(8,128)(2,1)}) custom-call(s32[6,1,64]{2,1,0:T(1,128)} %bitcast.6, s32[6,1,64]{2,1,0:T(1,128)} %bitcast.7, bf16[64,6,128,128]{3,2,1,0:T(8,128)(2,1)} %bitcast.5, bf16[512,128]{1,0:T(8,128)(2,1)} %feat_hbm.1, bf16[128,256]{1,0:T(8,128)(2,1)} %weight_hbm.1, ...), custom_call_target="tpu_custom_call" | custom-call | tf_op jit(solution)/shard_map/graph_layer/pallas_call | solution.py:513
  98.6 1.8 %results.1 = (bf16[512,256]{1,0:T(8,128)(2,1)}, f32[128,256]{1,0:T(8,128)}, bf16[512,128]{1,0:T(8,128)(2,1)}) custom-call(bf16[512,256]{1,0:T(8,128)(2,1)} %get-tuple-element.6.refs_0_, f32[128,256]{1,0:T(8,128)} %get-tuple-element.7.refs_1_, bf16[512,128]{1,0:T(8,128)(2,1)} %get-tuple-element.8.refs_2_), custom_call_target="tpu_custom_call" | custom-call | tf_op jit(solution)/shard_map/results/pallas_call | solution.py:543

commit v3 on v2

--- a/solution.py
+++ b/solution.py
@@ -20,9 +20,12 @@
 EMPTY = SLOTS
 ZERO = TILES
 FWD_ORDER = (3, 2, 1, 0)
-TURNS = ((0, 0), (0, 1), (3, 0), (1, 0), (0, 2), (0, 3), (3, 1), (1, 1), (3, 2), (1, 2), (3, 3), (1, 3))
-TURNS += ((2, 0), (2, 1), (2, 2), (2, 3))
-N_COPIES = 160
+TURNS = ((0, 0, 0), (0, 0, 1), (1, 0, 0), (0, 3, 0), (0, 1, 0), (0, 0, 2), (0, 0, 3), (1, 0, 1))
+TURNS += ((0, 3, 1), (0, 1, 1), (1, 3, 0), (1, 1, 0), (1, 0, 2), (1, 0, 3))
+TURNS += ((0, 3, 2), (0, 1, 2), (0, 3, 3), (0, 1, 3), (1, 3, 1), (1, 1, 1))
+TURNS += ((1, 3, 2), (1, 1, 2), (1, 3, 3), (1, 1, 3))
+TURNS += tuple((half, 2, mask) for half in (0, 1) for mask in range(4))
+N_COPIES = 224
 N_LOADS = 8
 LAST = 6
 INDEX = 8
@@ -183,8 +186,8 @@
         copy.wait_recv()
     got_places.wait()
 
-    def product(y, z):
-        first = (mod4(my + y) * 4 + masked(ml, z)) * B
+    def product(half, y, z):
+        first = (mod4(my + y) * 4 + masked(ml, z)) * B + 2 * half
 
         def tile(r):
             acc = jnp.zeros((T, T), F32)
@@ -196,7 +199,7 @@
                 acc = acc + jnp.dot(lhs, rhs, preferred_element_type=F32)
             parts[r] = acc.astype(BF)
 
-        for t in range(B):
+        for t in range(2):
             tile(first + t)
         return first
 
@@ -204,42 +207,38 @@
         where = pl.ds(first, count)
         ref[where] = (ref[where].astype(F32) + other.astype(F32)).astype(BF)
 
-    ups1, downs1, ups2, downs2, zs = [], [], [], [], []
-    for q in range(4):
-        first = product(2, FWD_ORDER[q])
-        ups1.append(net.send(blocks(parts, first, 2), up1.at[q], y=1))
-        downs1.append(net.send(blocks(parts, first + 2, 2), down1.at[q], y=3))
-    def second(q):
-        first = product(1, FWD_ORDER[q])
-        ups1[q].wait_recv()
-        add_to(parts, first, 2, up1[q])
-        ups2.append(net.send(blocks(parts, first, B), up2.at[q], y=1))
-        first = product(3, FWD_ORDER[q])
-        downs1[q].wait_recv()
-        add_to(parts, first + 2, 2, down1[q])
-        downs2.append(net.send(blocks(parts, first, B), down2.at[q], y=3))
-
-    def third(q):
-        first = product(0, FWD_ORDER[q])
-        ups2[q].wait_recv()
-        downs2[q].wait_recv()
-        here = parts[pl.ds(first, B)].astype(F32) + up2[q].astype(F32) + down2[q].astype(F32)
+    ups1, downs1, ups2, downs2, zs = {}, {}, {}, {}, {}
+
+    def first(h, pair):
+        for q, place in [(q, product(h, 2, FWD_ORDER[q])) for q in pair]:
+            ups1[h, q] = net.send(blocks(parts, place, 1), blocks(up1.at[q], h, 1), y=1)
+            downs1[h, q] = net.send(blocks(parts, place + 1, 1), blocks(down1.at[q], h, 1), y=3)
+
+    def second(h, q):
+        two = pl.ds(2 * h, 2)
+        right, left = product(h, 1, FWD_ORDER[q]), product(h, 3, FWD_ORDER[q])
+        ups1[h, q].wait_recv()
+        add_to(parts, right, 1, up1[q, pl.ds(h, 1)])
+        ups2[h, q] = net.send(blocks(parts, right, 2), up2.at[q, two], y=1)
+        downs1[h, q].wait_recv()
+        add_to(parts, left + 1, 1, down1[q, pl.ds(h, 1)])
+        downs2[h, q] = net.send(blocks(parts, left, 2), down2.at[q, two], y=3)
+
+    def own(h):
+        for q in range(4):
+            product(h, 0, FWD_ORDER[q])
+
+    def third(h, q):
+        two = pl.ds(2 * h, 2)
+        place = (my * 4 + masked(ml, FWD_ORDER[q])) * B + 2 * h
+        ups2[h, q].wait_recv()
+        downs2[h, q].wait_recv()
+        here = parts[pl.ds(place, 2)].astype(F32) + up2[q, two].astype(F32) + down2[q, two].astype(F32)
         if q < 3:
-            zsend[q] = here.astype(BF)
-            zs.append(net.send(zsend.at[q], zrecv.at[q], z=FWD_ORDER[q]))
+            zsend[q, two] = here.astype(BF)
+            zs[h, q] = net.send(zsend.at[q, two], zrecv.at[q, two], z=FWD_ORDER[q])
         else:
-            total[...] = here
-
-    second(0)
-    second(1)
-    second(2)
-    third(0)
-    second(3)
-    third(1)
-    third(2)
-    third(3)
-    for copy in zs:
-        copy.wait_recv()
+            total[two] = here
 
     got_rowdeg.wait()
     got_weight.wait()
@@ -247,28 +246,29 @@
     row_scale = lax.rsqrt(rowdeg_ref[...].astype(F32))
     weight = weight_ref[...]
     lean = math.sqrt(2.0 / math.pi)
-    for t in range(B):
-        rows = pl.ds(t * T, T)
-        aggregate = total[t]
+    def dense(h):
         for q in range(3):
-            aggregate = aggregate + zrecv[q, t].astype(F32)
-        smoothed = (aggregate * down_rows(row_scale, t)).astype(BF)
-        pre = jnp.dot(smoothed, weight, preferred_element_type=F32)
-        square = pre * pre
-        slope = jnp.tanh(lean * pre * (1.0 + 0.044715 * square))
-        gate = 0.5 * (1.0 + slope)
-        hidden_ref[rows, :] = (pre * gate).astype(BF)
-        steep = gate + 0.5 * pre * (1.0 - slope * slope) * (lean * (1.0 + 3.0 * 0.044715 * square))
-        grad_pre = (cot_ref[rows, :].astype(F32) * steep).astype(BF)
-        spread = lax.dot_general(weight, grad_pre, (((1,), (1,)), ((), ())), preferred_element_type=F32)
-        gpanel[col * B + t] = (spread * row_scale[t : t + 1, :]).astype(BF)
-        outer = lax.dot_general(smoothed, grad_pre, (((0,), (0,)), ((), ())), preferred_element_type=F32)
-        if t == 0:
-            wlocal[...] = outer
-        else:
-            wlocal[...] += outer
-
-    put_hidden = move(hidden_ref, hidden_hbm)
+            zs[h, q].wait_recv()
+        for t in (2 * h, 2 * h + 1):
+            rows = pl.ds(t * T, T)
+            aggregate = total[t]
+            for q in range(3):
+                aggregate = aggregate + zrecv[q, t].astype(F32)
+            smoothed = (aggregate * down_rows(row_scale, t)).astype(BF)
+            pre = jnp.dot(smoothed, weight, preferred_element_type=F32)
+            square = pre * pre
+            slope = jnp.tanh(lean * pre * (1.0 + 0.044715 * square))
+            gate = 0.5 * (1.0 + slope)
+            hidden_ref[rows, :] = (pre * gate).astype(BF)
+            steep = gate + 0.5 * pre * (1.0 - slope * slope) * (lean * (1.0 + 3.0 * 0.044715 * square))
+            grad_pre = (cot_ref[rows, :].astype(F32) * steep).astype(BF)
+            spread = lax.dot_general(weight, grad_pre, (((1,), (1,)), ((), ())), preferred_element_type=F32)
+            gpanel[col * B + t] = (spread * row_scale[t : t + 1, :]).astype(BF)
+            outer = lax.dot_general(smoothed, grad_pre, (((0,), (0,)), ((), ())), preferred_element_type=F32)
+            if t == 0:
+                wlocal[...] = outer
+            else:
+                wlocal[...] += outer
 
     def grads_at(y, z, first=0, count=B):
         place = mod4(my + y) * 4 + masked(ml, z)
@@ -278,8 +278,8 @@
         ref = grads_at(dy, dz, first, count)
         return net.send(ref, ref, **shift)
 
-    def back(y, z):
-        first = (mod4(my + y) * 4 + masked(ml, z)) * B
+    def back(half, y, z):
+        first = (mod4(my + y) * 4 + masked(ml, z)) * B + 2 * half
 
         def tile(r):
             grads = gpanel[r]
@@ -292,66 +292,121 @@
                 chain[slot] = one
                 chain[slot + 1] = two
 
-        for t in range(B):
+        for t in range(2):
             tile(first + t)
 
-    gups, gdowns, fups, fdowns = [], [], [], []
-
-    def along(mask):
-        gups.append(hand_on(0, mask, 0, B, y=1))
-        gdowns.append(hand_on(0, mask, 0, B, y=3))
-
-    def forward(mask):
-        gups[mask].wait_recv()
-        fups.append(hand_on(-1, mask, 0, 2, y=1))
-        gdowns[mask].wait_recv()
-        fdowns.append(hand_on(1, mask, 2, 2, y=3))
-
-    along(0)
-    gz = [None] + [hand_on(0, 0, 0, B, z=mask) for mask in (1, 2, 3)]
+    gups, gdowns, fups, fdowns, gz = {}, {}, {}, {}, {}
+
+    def along(h, mask):
+        if mask > 0:
+            gz[h, mask].wait_recv()
+        gups[h, mask] = hand_on(0, mask, 2 * h, 2, y=1)
+        gdowns[h, mask] = hand_on(0, mask, 2 * h, 2, y=3)
+
+    def forward(h, mask):
+        gups[h, mask].wait_recv()
+        fups[h, mask] = hand_on(-1, mask, 2 * h, 1, y=1)
+        gdowns[h, mask].wait_recv()
+        fdowns[h, mask] = hand_on(1, mask, 2 * h + 1, 1, y=3)
+
+    def over_z(h):
+        for mask in (1, 2, 3):
+            gz[h, mask] = hand_on(0, 0, 2 * h, 2, z=mask)
+
+    def beside_back(h, mask):
+        back(h, 3, mask)
+        back(h, 1, mask)
+
+    first(0, (0, 1))
+    first(0, (2, 3))
+    second(0, 0)
+    second(0, 1)
+    first(1, (0, 1))
+    first(1, (2, 3))
+    second(0, 2)
+    second(0, 3)
+    own(0)
+    third(0, 0)
+    second(1, 0)
+    third(0, 1)
+    second(1, 1)
+    third(0, 2)
+    second(1, 2)
+    third(0, 3)
+    second(1, 3)
+    own(1)
+    third(1, 0)
+    dense(0)
+    along(0, 0)
+    third(1, 1)
+    third(1, 2)
+    over_z(0)
+    third(1, 3)
+    back(0, 0, 0)
+    along(0, 1)
+    dense(1)
+    along(1, 0)
+    over_z(1)
+    put_hidden = move(hidden_ref, hidden_hbm)
     wys = [
         net.send(wlocal.at[pl.ds(mod4(my + d) * 32, 32)], wy.at[d - 1], y=d) for d in (1, 2, 3)
     ]
-    back(0, 0)
-    gz[1].wait_recv()
-    along(1)
-    back(0, 1)
-    forward(0)
-    back(3, 0)
-    back(1, 0)
-    gz[2].wait_recv()
-    along(2)
-    back(0, 2)
-    gz[3].wait_recv()
-    along(3)
-    back(0, 3)
-    forward(1)
+    forward(0, 0)
+    back(0, 0, 1)
+    back(1, 0, 0)
+    along(0, 2)
+    along(0, 3)
+    beside_back(0, 0)
+    back(0, 0, 2)
+    back(0, 0, 3)
+    along(1, 1)
+    forward(0, 1)
+    forward(1, 0)
+    back(1, 0, 1)
+    beside_back(0, 1)
+    beside_back(1, 0)
+    along(1, 2)
+    along(1, 3)
     for copy in wys:
         copy.wait_recv()
     wz[3] = wlocal[pl.ds(my * 32, 32), :] + wy[0] + wy[1] + wy[2]
     wzs = [
         net.send(wz.at[3, pl.ds(masked(ml, m) * 8, 8)], wz.at[m - 1, pl.ds(0, 8)], z=m) for m in (1, 2, 3)
     ]
-    back(3, 1)
-    back(1, 1)
-    forward(2)
-    back(3, 2)
-    back(1, 2)
-    forward(3)
-    back(3, 3)
-    back(1, 3)
+    back(1, 0, 2)
+    back(1, 0, 3)
+    forward(0, 2)
+    forward(0, 3)
+    beside_back(0, 2)
+    beside_back(0, 3)
+    forward(1, 1)
+    forward(1, 2)
+    beside_back(1, 1)
+    beside_back(1, 2)
     for copy in wzs:
         copy.wait_recv()
     wx[mx] = wz[3, pl.ds(ml * 8, 8), :] + wz[0, :8, :] + wz[1, :8, :] + wz[2, :8, :]
     wxs = [net.send(wx.at[mx], wx.at[mx], x=d) for d in (1, 2, 3)]
+    forward(1, 3)
+    beside_back(1, 3)
     for mask in range(4):
-        fups[mask].wait_recv()
-        fdowns[mask].wait_recv()
-        back(2, mask)
+        fups[0, mask].wait_recv()
+        fdowns[0, mask].wait_recv()
+    for mask in range(4):
+        back(0, 2, mask)
     for copy in wxs:
         copy.wait_recv()
     wc[0] = wx[0] + wx[1] + wx[2] + wx[3]
     wcs = net.send(wc.at[0], wc.at[1], core=1)
+    for pair in ((0, 1), (2, 3)):
+        for mask in pair:
+            fups[1, mask].wait_recv()
+            fdowns[1, mask].wait_recv()
+        for mask in pair:
+            back(1, 2, mask)
+    wcs.wait_recv()
+    wh[0] = wc[0] + wc[1]
+    whs = net.send(wh.at[0], wh.at[1], half=1)
 
     def column(half, x, core):
         return (lax.rem(mz + half, 2) * 8 + mod4(mx + x) * 2 + lax.rem(mc + core, 2)) * B
@@ -407,28 +462,23 @@
     chip_sum(2)
     beside(0, 0)
     beside(0, 2)
-    chip_sum(4)
-    opposite(1, 0)
-    opposite(1, 2)
-    wcs.wait_recv()
-    wh[0] = wc[0] + wc[1]
-    whs = net.send(wh.at[0], wh.at[1], half=1)
-    chip_sum(3)
-    cross(0)
-    chip_sum(5)
-    chip_sum(6)
-    beside(1, 0)
-    cross(2)
-    beside(1, 2)
-    chip_sum(7)
-
     whs.wait_recv()
     wrows = my * 32 + ml * 8
     wfull[pl.ds(wrows, 8), :] = (wh[0] + wh[1]) * grad_scale
     wzs2 = [
-        net.send(wfull.at[pl.ds(wrows, 8)], wfull.at[pl.ds(wrows, 8)], z=d) for d in (1, 2, 3)
+        net.send(wfull.at[pl.ds(wrows, 8)], wfull.at[pl.ds(wrows, 8)], z=m) for m in (1, 2, 3)
     ]
-
+    chip_sum(4)
+    opposite(1, 0)
+    opposite(1, 2)
+    chip_sum(3)
+    cross(0)
+    cross(2)
+    chip_sum(5)
+    chip_sum(6)
+    beside(1, 0)
+    beside(1, 2)
+    chip_sum(7)
     for copy in wzs2:
         copy.wait_recv()
     wband = wfull.at[pl.ds(my * 32, 32)]
@@ -455,10 +505,11 @@
     def turn_of(r):
         dy = mod4(r // 16 - my)
         z = lax.rem(r // 4, 4)
+        part = lax.rem(r // 2, 2)
         turn = jnp.zeros_like(r)
-        for n, (y, mask) in enumerate(TURNS):
-            turn = jnp.where((dy == y) & (z == masked(ml, mask)), n, turn)
-        return turn * B + lax.rem(r, B)
+        for n, (half, y, mask) in enumerate(TURNS):
+            turn = jnp.where((part == half) & (dy == y) & (z == masked(ml, mask)), n, turn)
+        return turn * 2 + lax.rem(r, 2)
 
     over = lax.broadcasted_iota(jnp.int32, square, 1)
     down = lax.broadcasted_iota(jnp.int32, square, 0)

time: 100 us -> 95.9 us (0.959)
  Pallas kernels: 99.8 us -> 95.1 us
    pallas_call x1, Pallas kernels: 97.9 us -> 93.3 us  [body(): pl.pallas_call(functools.partial(kernel, grad_scale), out_shape=shapes, i...]
where the time goes in v3:
time: 95.9 us; the launch traced here: 95.8 us
  Pallas kernels  95.1 us (99%)
    pallas_call x1, Pallas kernels, body(): pl.pallas_call(functools.partial(kernel, grad_scale), out_shape=shapes, i...  93.3 us

profile of v3, /device:TPU:1, one launch (start us, length us, event | category | flops | bytes accessed | tf_op | source)
XLA Modules:
  0.0 95.8 jit_solution(10255044016066935124)
XLA Ops:
  0.6 93.3 %graph_layer.1 = (bf16[512,256]{1,0:T(8,128)(2,1)}, f32[128,256]{1,0:T(8,128)}, bf16[512,128]{1,0:T(8,128)(2,1)}) custom-call(s32[6,1,64]{2,1,0:T(1,128)} %bitcast.6, s32[6,1,64]{2,1,0:T(1,128)} %bitcast.7, bf16[64,6,128,128]{3,2,1,0:T(8,128)(2,1)} %bitcast.5, bf16[512,128]{1,0:T(8,128)(2,1)} %feat_hbm.1, bf16[128,256]{1,0:T(8,128)(2,1)} %weight_hbm.1, ...), custom_call_target="tpu_custom_call" | custom-call | tf_op jit(solution)/shard_map/graph_layer/pallas_call | solution.py:564
  93.9 1.8 %results.1 = (bf16[512,256]{1,0:T(8,128)(2,1)}, f32[128,256]{1,0:T(8,128)}, bf16[512,128]{1,0:T(8,128)(2,1)}) custom-call(bf16[512,256]{1,0:T(8,128)(2,1)} %get-tuple-element.6.refs_0_, f32[128,256]{1,0:T(8,128)} %get-tuple-element.7.refs_1_, bf16[512,128]{1,0:T(8,128)(2,1)} %get-tuple-element.8.refs_2_), custom_call_target="tpu_custom_call" | custom-call | tf_op jit(solution)/shard_map/results/pallas_call | solution.py:594

commit v4 on v3

--- a/solution.py
+++ b/solution.py
@@ -48,9 +48,17 @@
     def __init__(self, send_sems, recv_sems):
         self.sems = (send_sems, recv_sems)
         self.made = []
+        self.seen = 0
         self.place = coords()
-
-    def device(self, x=0, y=0, z=0, core=0, half=0):
+        self.devices = {}
+
+    def device(self, **shift):
+        key = tuple(sorted(shift.items()))
+        if key not in self.devices:
+            self.devices[key] = self.find(**shift)
+        return self.devices[key]
+
+    def find(self, x=0, y=0, z=0, core=0, half=0):
         mz, mx, mc, my, ml = self.place
         row = lax.rem(mz + half, 2) * 8 + mod4(mx + x) * 2 + lax.rem(mc + core, 2)
         return (row, mod4(my + y) * 4 + masked(ml, z))
@@ -68,6 +76,11 @@
         copy.start()
         self.made.append(copy)
         return copy
+
+    def drain(self, count):
+        for copy in self.made[self.seen : count]:
+            copy.wait_send()
+        self.seen = count
 
 
 PEERS = (
@@ -185,6 +198,8 @@
     for copy in from_core:
         copy.wait_recv()
     got_places.wait()
+
+    gathers = len(net.made)
 
     def product(half, y, z):
         first = (mod4(my + y) * 4 + masked(ml, z)) * B + 2 * half
@@ -336,6 +351,7 @@
     second(1, 3)
     own(1)
     third(1, 0)
+    net.drain(gathers)
     dense(0)
     along(0, 0)
     third(1, 1)
@@ -343,6 +359,7 @@
     over_z(0)
     third(1, 3)
     back(0, 0, 0)
+    forward(0, 0)
     along(0, 1)
     dense(1)
     along(1, 0)
@@ -351,7 +368,6 @@
     wys = [
         net.send(wlocal.at[pl.ds(mod4(my + d) * 32, 32)], wy.at[d - 1], y=d) for d in (1, 2, 3)
     ]
-    forward(0, 0)
     back(0, 0, 1)
     back(1, 0, 0)
     along(0, 2)
@@ -411,6 +427,7 @@
     def column(half, x, core):
         return (lax.rem(mz + half, 2) * 8 + mod4(mx + x) * 2 + lax.rem(mc + core, 2)) * B
 
+    before_sums = len(net.made)
     order = [(half, x) for half in (1, 0) for x in (2, 1, 3, 0)]
     cores = []
     for n, (half, x) in enumerate(order):
@@ -483,19 +500,21 @@
         copy.wait_recv()
     wband = wfull.at[pl.ds(my * 32, 32)]
     wys2 = [net.send(wband, wband, y=d) for d in (1, 2, 3)]
+    net.drain(before_sums)
+    puts = [put_hidden]
     for t, copy in zip(halves, across):
         here = gathered(1, t)
         copy.wait_recv()
         for u in range(2):
             tile = here[u] + hrecv[t + u].astype(F32)
             fgrad_ref[pl.ds((t + u) * T, T), :] = (tile * col_scale[t + u : t + u + 1, :]).T.astype(BF)
-    put_fgrad = move(fgrad_ref, fgrad_hbm)
+        part = pl.ds(t * T, 2 * T)
+        puts.append(move(fgrad_ref.at[part], fgrad_hbm.at[part]))
     for copy in wys2:
         copy.wait_recv()
-    put_wgrad = move(wfull, wgrad_hbm)
-    for copy in net.made:
-        copy.wait_send()
-    for put in (put_hidden, put_fgrad, put_wgrad):
+    puts.append(move(wfull, wgrad_hbm))
+    net.drain(len(net.made))
+    for put in puts:
         put.wait()
 
 

time: 95.9 us -> 95.2 us (level)
  Pallas kernels: 95.1 us -> 93.6 us
    pallas_call x1, Pallas kernels: 93.3 us -> 91.8 us  [body(): pl.pallas_call(functools.partial(kernel, grad_scale), out_shape=shapes, i...]
where the time goes in v4:
time: 95.2 us; the launch traced here: 94.2 us
  Pallas kernels  93.6 us (98%)
    pallas_call x1, Pallas kernels, body(): pl.pallas_call(functools.partial(kernel, grad_scale), out_shape=shapes, i...  91.8 us

profile of v4, /device:TPU:1, one launch (start us, length us, event | category | flops | bytes accessed | tf_op | source)
XLA Modules:
  0.0 94.2 jit_solution(17208092014913322995)
XLA Ops:
  0.6 91.8 %graph_layer.1 = (bf16[512,256]{1,0:T(8,128)(2,1)}, f32[128,256]{1,0:T(8,128)}, bf16[512,128]{1,0:T(8,128)(2,1)}) custom-call(s32[6,1,64]{2,1,0:T(1,128)} %bitcast.6, s32[6,1,64]{2,1,0:T(1,128)} %bitcast.7, bf16[64,6,128,128]{3,2,1,0:T(8,128)(2,1)} %bitcast.5, bf16[512,128]{1,0:T(8,128)(2,1)} %feat_hbm.1, bf16[128,256]{1,0:T(8,128)(2,1)} %weight_hbm.1, ...), custom_call_target="tpu_custom_call" | custom-call | tf_op jit(solution)/shard_map/graph_layer/pallas_call | solution.py:583
  92.4 1.8 %results.1 = (bf16[512,256]{1,0:T(8,128)(2,1)}, f32[128,256]{1,0:T(8,128)}, bf16[512,128]{1,0:T(8,128)(2,1)}) custom-call(bf16[512,256]{1,0:T(8,128)(2,1)} %get-tuple-element.6.refs_0_, f32[128,256]{1,0:T(8,128)} %get-tuple-element.7.refs_1_, bf16[512,128]{1,0:T(8,128)(2,1)} %get-tuple-element.8.refs_2_), custom_call_target="tpu_custom_call" | custom-call | tf_op jit(solution)/shard_map/results/pallas_call | solution.py:613
